TPU v7x, 512 devices: a whole 4x4x16 slice. The times are simulated.
512 devices in a mesh: row: 32 (over z_lo, y), col: 16 (over z_hi, x, core).
Axes of the slice: x: 4, y: 4, z: 16 (z_hi: 2, z_lo: 8; z = z_hi * 8 + z_lo), core: 2. Of those that a mesh axis runs over, the one named last changes fastest.
Arguments:
- entries: int32 [128, 64, 128, 128], P('row', 'col'), may hold values from -2 to 2
- tile_cols: int32 [128, 64], P('row', 'col'), may hold values from 0 to 31
- block_now: int32 [32, 65536], P(None, ('col', 'row')), may hold values from 0 to 65520
- block_prev: int32 [32, 65536], P(None, ('col', 'row')), may hold values from 0 to 65520
- block_prev2: int32 [32, 65536], P(None, ('col', 'row')), may hold values from 0 to 65520
- gram_prev: int32 [32, 32], replicated, may hold values from 0 to 65520
- square_prev: int32 [32, 32], replicated, may hold values from 0 to 65520
- inverse_prev: int32 [32, 32], replicated, may hold values from 0 to 65520
- inverse_prev2: int32 [32, 32], replicated, may hold values from 0 to 65520
Outputs:
- next_block: float32 [32, 65536], P(None, ('col', 'row'))
- later_block: float32 [32, 65536], P(None, ('col', 'row'))
Inputs may be any that keep to these rules, and one draw needn't show every extreme that they name: `tile_cols`: stored tiles that name the same tile column in one tile row add. `block_prev`: residues. `block_prev2`: residues. `gram_prev`: residues. `square_prev`: residues. `inverse_prev`: residues. `inverse_prev2`: residues.
All inputs are finite; a program needn't handle non-finite values.
Results may differ from a plain program's by a relative error of at most 0.0003.
Values sent between devices are 32-bit elements; how exact they have to be, the bound alone decides.
No kernel may reach another device: no remote copies, remote signals or barrier semaphores. Data moves between devices by JAX's collectives and lax.ppermute only.
A program may use at most 64 MiB of HBM per device.

v0:
```python
import jax
import jax.numpy as jnp
from jax import lax
from jax.sharding import PartitionSpec as P

modulus = 65521.0


def residue(values):
    return jnp.mod(values, modulus)


def split_digits(values):
    top_part = jnp.floor(values / 256.0)
    return (top_part, values - top_part * 256.0)


def fold_digits(top_sum, low_sum):
    return residue(residue(residue(top_sum) * 256.0) + residue(low_sum))


def fold_three(upper_part, middle, lower_part):
    return residue(
        residue(residue(upper_part) * 15.0) + residue(residue(middle) * 256.0) + residue(lower_part)
    )


def mulmod(left_side, right_side):
    top_part, low_part = split_digits(right_side)
    return fold_digits(left_side * top_part, left_side * low_part)


def exact_dot(left_side, right_side):
    return jnp.dot(
        left_side, right_side, precision=lax.Precision.HIGHEST, preferred_element_type=jnp.float32
    )


def small_product(left_side, right_side):
    left_top, left_low = split_digits(left_side)
    right_top, right_low = split_digits(right_side)
    return fold_three(
        exact_dot(left_top, right_top),
        exact_dot(left_top, right_low) + exact_dot(left_low, right_top),
        exact_dot(left_low, right_low),
    )


def inverse_scalar(number):
    result = jnp.ones_like(number)
    square = number
    exponent = 65519
    for position in range(16):
        if exponent >> position & 1:
            result = mulmod(result, square)
        square = mulmod(square, square)
    return result


def inverse_matrix(matrix):
    matrix_order = matrix.shape[0]
    augmented = jnp.concatenate([matrix, jnp.eye(matrix_order, dtype=matrix.dtype)], axis=1)
    row_numbers = jnp.arange(matrix_order, dtype=jnp.int32)

    def eliminate(column, augmented):
        column = jnp.asarray(column).astype(jnp.int32)
        pivot_column = augmented[:, column]
        usable = (pivot_column != 0.0) & (row_numbers >= column)
        pivot_row_id = jnp.where(jnp.any(usable), jnp.argmax(usable), column)
        pivot_row = augmented[pivot_row_id]
        current_row = augmented[column]
        swapped = jnp.where(
            (row_numbers == column)[:, None],
            pivot_row[None, :],
            jnp.where((row_numbers == pivot_row_id)[:, None], current_row[None, :], augmented),
        )
        scaled = mulmod(pivot_row, inverse_scalar(pivot_row[column]))
        factors = jnp.where(row_numbers == column, 0.0, swapped[:, column])
        reduced = residue(swapped - mulmod(factors[:, None], scaled[None, :]) + modulus)
        return jnp.where((row_numbers == column)[:, None], scaled[None, :], reduced)

    augmented = lax.fori_loop(0, matrix_order, eliminate, augmented)
    return augmented[:, matrix_order:]


def coefficients(
    gram_now, square_now, inverse_now, inverse_prev, inverse_prev2, gram_old, square_old
):
    identity = jnp.eye(gram_now.shape[0], dtype=gram_now.dtype)
    first = residue(identity - small_product(residue(square_now + gram_now), inverse_now) + modulus)
    second = residue(modulus - small_product(gram_now, inverse_prev))
    middle = residue(identity - small_product(inverse_prev, gram_old) + modulus)
    third = residue(
        modulus
        - small_product(small_product(residue(square_old + gram_old), middle), inverse_prev2)
    )
    return jnp.concatenate([first, second, third], axis=1)


def digit_stack(values):
    top_part, low_part = split_digits(values)
    return jnp.stack([top_part, low_part]).astype(jnp.bfloat16)


def combine_blocks(coeffs, stacked):
    products = jnp.einsum(
        "dab,ebn->dean",
        digit_stack(coeffs),
        digit_stack(stacked),
        preferred_element_type=jnp.float32,
    )
    return fold_three(products[0, 0], products[0, 1] + products[1, 0], products[1, 1])


def gram_local(first, second):
    column_count = first.shape[1]
    group_width = min(column_count, 128)
    groups = column_count // group_width
    first_digits = digit_stack(first).reshape(2, first.shape[0], groups, group_width)
    second_digits = digit_stack(second).reshape(2, second.shape[0], groups, group_width)
    products = jnp.einsum(
        "dagw,ecgw->gdeac", first_digits, second_digits, preferred_element_type=jnp.float32
    )
    per_group = fold_three(
        products[:, 0, 0], products[:, 0, 1] + products[:, 1, 0], products[:, 1, 1]
    )
    return residue(jnp.sum(per_group, axis=0))


def digit_pair(values):
    top_part, low_part = split_digits(values)
    return jnp.stack([top_part, low_part])


def forward_partial(block_full, tile_values, tile_cols):
    tile_rows, slot_count, tile_size = (
        tile_values.shape[0],
        tile_values.shape[1],
        tile_values.shape[2],
    )
    block_rows = block_full.shape[0]
    top_part, low_part = split_digits(block_full)
    digits = jnp.concatenate([top_part, low_part], axis=0).astype(jnp.bfloat16)
    digits = digits.reshape(2 * block_rows, -1, tile_size)
    picked = jnp.take(digits, tile_cols.reshape(-1), axis=1).reshape(
        2 * block_rows, tile_rows, slot_count, tile_size
    )
    raw_sums = jnp.einsum("brsk,rsjk->brj", picked, tile_values, preferred_element_type=jnp.float32)
    return fold_digits(raw_sums[:block_rows], raw_sums[block_rows:]).reshape(
        block_rows, tile_rows * tile_size
    )


def backward_partial(projected, tile_values, onehot):
    tile_rows, tile_size = (tile_values.shape[0], tile_values.shape[2])
    block_rows = projected.shape[0]
    top_part, low_part = split_digits(projected)
    digits = (
        jnp.concatenate([top_part, low_part], axis=0)
        .astype(jnp.bfloat16)
        .reshape(2 * block_rows, tile_rows, tile_size)
    )
    spread = jnp.einsum("brj,rsjk->brsk", digits, tile_values, preferred_element_type=jnp.float32)
    raw_sums = jnp.einsum(
        "brsk,rsc->bck",
        spread,
        onehot,
        precision=lax.Precision.HIGHEST,
        preferred_element_type=jnp.float32,
    )
    return fold_digits(raw_sums[:block_rows], raw_sums[block_rows:]).reshape(block_rows, -1)


def body(
    entries,
    tile_cols,
    block_now,
    block_prev,
    block_prev2,
    gram_prev,
    square_prev,
    inverse_prev,
    inverse_prev2,
):
    tile_values = entries.astype(jnp.bfloat16)
    tile_size = tile_values.shape[2]
    share_width = block_now.shape[1]
    col_tiles = share_width * lax.axis_size("row") // tile_size
    onehot = (
        tile_cols[:, :, None] == jnp.arange(col_tiles, dtype=jnp.int32)[None, None, :]
    ).astype(jnp.float32)
    current = block_now.astype(jnp.float32)
    earlier = block_prev.astype(jnp.float32)
    earliest = block_prev2.astype(jnp.float32)
    gram_old = gram_prev.astype(jnp.float32)
    square_old = square_prev.astype(jnp.float32)
    inverse_old = inverse_prev.astype(jnp.float32)
    inverse_older = inverse_prev2.astype(jnp.float32)
    results = []
    for iteration in range(2):
        block_full = lax.all_gather(current, "row", axis=1, tiled=True)
        projected = residue(lax.psum(forward_partial(block_full, tile_values, tile_cols), "col"))
        partial_term = backward_partial(projected, tile_values, onehot)
        applied = residue(lax.psum_scatter(partial_term, "row", scatter_dimension=1, tiled=True))
        current_own = current
        both_sums = lax.psum(
            jnp.stack(
                [
                    digit_pair(gram_local(current_own, applied)),
                    digit_pair(gram_local(applied, applied)),
                ]
            ),
            ("row", "col"),
        )
        gram_now = fold_digits(both_sums[0, 0], both_sums[0, 1])
        square_now = fold_digits(both_sums[1, 0], both_sums[1, 1])
        inverse_now = inverse_matrix(gram_now)
        coeffs = coefficients(
            gram_now, square_now, inverse_now, inverse_old, inverse_older, gram_old, square_old
        )
        stacked = jnp.concatenate([current, earlier, earliest], axis=0)
        following = residue(applied + combine_blocks(coeffs, stacked))
        results.append(following / modulus)
        earliest, earlier, current = (earlier, current, following)
        inverse_older, inverse_old = (inverse_old, inverse_now)
        gram_old, square_old = (gram_now, square_now)
    return (results[0], results[1])


def solution(mesh):
    placed = (
        P("row", "col", None, None),
        P("row", "col"),
        P(None, ("col", "row")),
        P(None, ("col", "row")),
        P(None, ("col", "row")),
        P(),
        P(),
        P(),
        P(),
    )
    return jax.shard_map(
        body,
        mesh=mesh,
        in_specs=placed,
        out_specs=(P(None, ("col", "row")), P(None, ("col", "row"))),
        check_vma=False,
    )
```

profile of v0, /device:TPU:1, one launch (start us, length us, event | category | flops | bytes accessed | tf_op | source)
XLA Modules:
  0.0 2244.6 jit_solution(948067549384732013)
XLA Ops:
  7.2 0.8 reshape.1652
  8.8 114.7 %all_gather.6 = f32[32,4096]{1,0:T(8,128)S(1)} all-gather(f32[32,128]{1,0:T(8,128)S(1)} %get-tuple-element.319), channel_id=1, replica_groups=mesh['row'=32,'col'=16] {'row'}, dimensions={1}, use_global_device_ids=true | all-gather | bytes 540672 | tf_op jit(solution)/shard_map/all_gather | solution.py:201
  124.9 0.8 copy_bitcast_fusion.7
  129.3 247.2 %all-reduce.3.cloned.1.call-done = f32[32,512]{1,0:T(8,128)} async-done(((f32[32,512]{1,0:T(8,128)}), f32[32,512]{1,0:T(8,128)}) %all-reduce.3.cloned.1.call-update) | async-done | bytes 65552 | tf_op jit(solution)/shard_map/psum | solution.py:202
  376.5 0.9 fusion.102
  378.1 1.1 convolution_bitcast_fusion.1
  379.2 1.1 add_select_fusion.22
  380.3 1.1 copy.355
  383.5 212.7 %reduce-scatter.3.cloned.1.call-done = f32[32,128]{1,0:T(8,128)} async-done(((f32[32,4096]{1,0:T(8,128)}), f32[32,128]{1,0:T(8,128)}) %reduce-scatter.3.cloned.1.call-update) | async-done | bytes 16400 | tf_op jit(solution)/shard_map/reduce_scatter | solution.py:204
  596.2 0.7 fusion.339
  597.5 125.4 %psum.29 = f32[2,2,32,32]{2,3,1,0:T(8,128)S(1)} all-reduce(f32[2,2,32,32]{2,3,1,0:T(8,128)S(1)} %pad_maximum_fusion.2), channel_id=1, replica_groups=mesh['row'=32,'col'=16] {'row','col'}, use_global_device_ids=true, to_apply=%region_2.4 | all-reduce | flops 4096 | bytes 32768 | tf_op jit(solution)/shard_map/psum | solution.py:206
  722.9 403.5 %while.36 = (s32[]{:T(128)}, f32[32,64]{0,1:T(8,128)S(1)}, s32[]{:T(128)}, s32[]{:T(128)}, s32[]{:T(128)}, /*index=5*/s32[]{:T(128)}, s32[]{:T(128)}, f32[]{:T(128)}, f32[]{:T(128)}, f32[]{:T(128)}, /*index=10*/f32[]{:T(128)}) while((s32[]{:T(128)}, f32[32,64]{0,1:T(8,128)S(1)}, s32[]{:T(128)}, s32[]{:T(128)}, ...), condition=%wide.region_6.8_spmd.clone.clone, body=%wide.region_3.7_spmd.clone.clone.sunk | while | flops 87498 | bytes 50118 | solution.py:82
  723.6 0.7 iota_reduce_fusion.4
  736.2 0.7 iota_reduce_fusion.4
  748.8 0.7 iota_reduce_fusion.4
  761.4 0.7 iota_reduce_fusion.4
  774.0 0.7 iota_reduce_fusion.4
  786.7 0.7 iota_reduce_fusion.4
  799.3 0.7 iota_reduce_fusion.4
  811.9 0.7 iota_reduce_fusion.4
  824.5 0.7 iota_reduce_fusion.4
  837.1 0.7 iota_reduce_fusion.4
  849.7 0.7 iota_reduce_fusion.4
  862.3 0.7 iota_reduce_fusion.4
  874.9 0.7 iota_reduce_fusion.4
  887.5 0.7 iota_reduce_fusion.4
  900.1 0.7 iota_reduce_fusion.4
  912.7 0.7 iota_reduce_fusion.4
  925.3 0.7 iota_reduce_fusion.4
  938.0 0.7 iota_reduce_fusion.4
  950.6 0.7 iota_reduce_fusion.4
  963.2 0.7 iota_reduce_fusion.4
  975.8 0.7 iota_reduce_fusion.4
  988.4 0.7 iota_reduce_fusion.4
  1001.0 0.7 iota_reduce_fusion.4
  1013.6 0.7 iota_reduce_fusion.4
  1026.2 0.7 iota_reduce_fusion.4
  1038.8 0.7 iota_reduce_fusion.4
  1076.7 0.7 iota_reduce_fusion.4
  1101.9 0.7 iota_reduce_fusion.4
  1114.5 0.7 iota_reduce_fusion.4
  1129.8 103.1 %all_gather.7 = f32[32,4096]{1,0:T(8,128)S(1)} all-gather(f32[32,128]{1,0:T(8,128)S(1)} %get-tuple-element.280), channel_id=1, replica_groups=mesh['row'=32,'col'=16] {'row'}, dimensions={1}, use_global_device_ids=true | all-gather | bytes 540672 | tf_op jit(solution)/shard_map/all_gather | solution.py:201
  1234.2 0.8 copy_bitcast_fusion.6
  1235.6 249.9 %all-reduce.5.cloned.1.call-done = f32[32,512]{1,0:T(8,128)} async-done(((f32[32,512]{1,0:T(8,128)}), f32[32,512]{1,0:T(8,128)}) %all-reduce.5.cloned.1.call-update) | async-done | bytes 65552 | tf_op jit(solution)/shard_map/psum | solution.py:202
  1485.5 0.9 fusion.103
  1486.7 1.1 convolution_bitcast_fusion
  1487.7 1.1 add_select_fusion.18
  1488.9 1.1 copy.354
  1491.4 213.1 %reduce-scatter.5.cloned.1.call-done = f32[32,128]{1,0:T(8,128)} async-done(((f32[32,4096]{1,0:T(8,128)}), f32[32,128]{1,0:T(8,128)}) %reduce-scatter.5.cloned.1.call-update) | async-done | bytes 16400 | tf_op jit(solution)/shard_map/reduce_scatter | solution.py:204
  1704.5 0.7 fusion.343
  1705.8 125.7 %psum.31 = f32[2,2,32,32]{2,3,1,0:T(8,128)S(1)} all-reduce(f32[2,2,32,32]{2,3,1,0:T(8,128)S(1)} %pad_maximum_fusion.3), channel_id=1, replica_groups=mesh['row'=32,'col'=16] {'row','col'}, use_global_device_ids=true, to_apply=%region_9.11 | all-reduce | flops 4096 | bytes 32768 | tf_op jit(solution)/shard_map/psum | solution.py:206
  1831.6 403.5 %while.37 = (s32[]{:T(128)}, f32[32,64]{0,1:T(8,128)S(1)}, s32[]{:T(128)}, s32[]{:T(128)}, s32[]{:T(128)}, /*index=5*/s32[]{:T(128)}, s32[]{:T(128)}, f32[]{:T(128)}, f32[]{:T(128)}, f32[]{:T(128)}, /*index=10*/f32[]{:T(128)}) while((s32[]{:T(128)}, f32[32,64]{0,1:T(8,128)S(1)}, s32[]{:T(128)}, s32[]{:T(128)}, ...), condition=%wide.region_13.15_spmd.clone.clone, body=%wide.region_10.14_spmd.clone.clone.sunk | while | flops 87498 | bytes 50118 | solution.py:82
  1832.2 0.7 iota_reduce_fusion.5
  1844.8 0.7 iota_reduce_fusion.5
  1983.5 0.7 iota_reduce_fusion.5
  1996.1 0.7 iota_reduce_fusion.5
  2008.8 0.7 iota_reduce_fusion.5
  2021.4 0.7 iota_reduce_fusion.5
  2034.0 0.7 iota_reduce_fusion.5
  2046.6 0.7 iota_reduce_fusion.5
  2059.2 0.7 iota_reduce_fusion.5
  2071.8 0.7 iota_reduce_fusion.5
  2084.4 0.7 iota_reduce_fusion.5
  2223.1 0.7 iota_reduce_fusion.5
  (674 shorter events, 155.7 us)
Async XLA Ops:
  7.2 116.5 %copy-start = (s32[4,4,128,128]{3,2,1,0:T(8,128)S(1)}, s32[4,4,128,128]{3,2,1,0:T(8,128)}, u32[]{:S(2)}) copy-start(s32[4,4,128,128]{3,2,1,0:T(8,128)} %param.15) | copy-start | bytes 3145732
  7.2 369.3 %all-reduce.3.cloned.1.call-start = ((), (), s32[]{:S(2)}) async-start(), calls=%async_computation.2 | async-start | bytes 131072 | tf_op jit(solution)/shard_map/psum | solution.py:202
  125.7 0.7 copy-start.5
  125.7 0.8 copy-start.6
  125.7 470.4 %reduce-scatter.3.cloned.1.call-start = ((), (), s32[]{:S(2)}) async-start(), calls=%async_computation.3 | async-start | bytes 540672 | tf_op jit(solution)/shard_map/reduce_scatter | solution.py:204
  126.9 0.7 copy-start.7
  128.2 0.7 copy-start.8
  377.4 0.7 copy-start.4
  381.5 1104.0 %all-reduce.5.cloned.1.call-start = ((), (), s32[]{:S(2)}) async-start(), calls=%async_computation.4 | async-start | bytes 131072 | tf_op jit(solution)/shard_map/psum | solution.py:202
  382.0 0.7 copy-start.9
  382.0 0.7 copy-start.10
  382.8 0.7 copy-start.1
  1129.0 0.7 copy-start.2
  1235.0 469.5 %reduce-scatter.5.cloned.1.call-start = ((), (), s32[]{:S(2)}) async-start(), calls=%async_computation.5 | async-start | bytes 540672 | tf_op jit(solution)/shard_map/reduce_scatter | solution.py:204
  2236.6 0.7 copy-start.3
Sparse Core Ops, SparseCore 0:
  125.8 250.6 all-reduce.2
  381.6 214.5 reduce-scatter.2
  1235.1 250.3 all-reduce.4
  1490.1 214.3 reduce-scatter.4
where the time goes:
time: 2250 us; the launch traced here: 2240 us
  waiting for transfers between devices  923 us (41%)
  loops' own time  641 us (28%)
  blocking collectives  469 us (21%)
  other arithmetic  139 us (6%)
  local copies, waits for them, and re-layouts  47.5 us (2%)
    another operation x2, loops' own time, inverse_matrix(): augmented = lax.fori_loop(0, matrix_order, eliminate, augmented)  641 us
    psum x2, waiting for transfers between devices, body(): lax.psum(forward_partial(block_full, tile_values, tile_cols), 'col')  497 us
    reduce_scatter x2, waiting for transfers between devices, body(): lax.psum_scatter(partial_term, 'row', scatter_dimension=1, tiled=True)  426 us
    psum x2, blocking collectives, body(): lax.psum(jnp.stack([digit_pair(gram_local(current_own, applied)), digit_p...  251 us
    all_gather x2, blocking collectives, body(): block_full = lax.all_gather(current, 'row', axis=1, tiled=True)  218 us
    another operation x64, other arithmetic, eliminate(): pivot_row_id = jnp.where(jnp.any(usable), jnp.argmax(usable), column)  46.5 us
  transfers between devices with their start and end apart: 4, of which 4 were waited for; matrix products, arithmetic and copies ran while one was open for 0% of the time, Pallas kernels for 0%

commit v1 on v0

--- a/solution.py
+++ b/solution.py
@@ -204,13 +204,16 @@
         applied = residue(lax.psum_scatter(partial_term, "row", scatter_dimension=1, tiled=True))
         current_own = current
         both_sums = lax.psum(
-            jnp.stack(
-                [
-                    digit_pair(gram_local(current_own, applied)),
-                    digit_pair(gram_local(applied, applied)),
-                ]
+            lax.psum(
+                jnp.stack(
+                    [
+                        digit_pair(gram_local(current_own, applied)),
+                        digit_pair(gram_local(applied, applied)),
+                    ]
+                ),
+                "row",
             ),
-            ("row", "col"),
+            "col",
         )
         gram_now = fold_digits(both_sums[0, 0], both_sums[0, 1])
         square_now = fold_digits(both_sums[1, 0], both_sums[1, 1])

time: 2250 us -> 2740 us (1.22)
  blocking collectives: 469 us -> 936 us
    psum x0 -> x2, blocking collectives: none -> 327 us  [body(): lax.psum(lax.psum(jnp.stack([digit_pair(gram_local(current_own, applied))...]
    psum x2, blocking collectives: 251 us -> 394 us  [body(): lax.psum(jnp.stack([digit_pair(gram_local(current_own, applied)), digit_p...]
where the time goes in v1:
time: 2740 us; the launch traced here: 2730 us
  waiting for transfers between devices  939 us (34%)
  blocking collectives  936 us (34%)
  loops' own time  641 us (23%)
  other arithmetic  139 us (5%)
  local copies, waits for them, and re-layouts  47.5 us (2%)
    another operation x2, loops' own time, inverse_matrix(): augmented = lax.fori_loop(0, matrix_order, eliminate, augmented)  641 us
    psum x2, waiting for transfers between devices, body(): lax.psum(forward_partial(block_full, tile_values, tile_cols), 'col')  513 us
    reduce_scatter x2, waiting for transfers between devices, body(): lax.psum_scatter(partial_term, 'row', scatter_dimension=1, tiled=True)  426 us
    psum x2, blocking collectives, body(): lax.psum(jnp.stack([digit_pair(gram_local(current_own, applied)), digit_p...  394 us
    psum x2, blocking collectives, body(): lax.psum(lax.psum(jnp.stack([digit_pair(gram_local(current_own, applied))...  327 us
    all_gather x2, blocking collectives, body(): block_full = lax.all_gather(current, 'row', axis=1, tiled=True)  215 us
  transfers between devices with their start and end apart: 4, of which 4 were waited for; matrix products, arithmetic and copies ran while one was open for 0% of the time, Pallas kernels for 0%

profile of v1, /device:TPU:1, one launch (start us, length us, event | category | flops | bytes accessed | tf_op | source)
XLA Modules:
  0.0 2727.5 jit_solution(17191804199030291254)
XLA Ops:
  7.2 0.8 reshape.1652
  8.8 114.7 %all_gather.6 = f32[32,4096]{1,0:T(8,128)S(1)} all-gather(f32[32,128]{1,0:T(8,128)S(1)} %get-tuple-element.319), channel_id=1, replica_groups=mesh['row'=32,'col'=16] {'row'}, dimensions={1}, use_global_device_ids=true | all-gather | bytes 540672 | tf_op jit(solution)/shard_map/all_gather | solution.py:201
  124.9 0.8 copy_bitcast_fusion.7
  129.3 247.2 %all-reduce.3.cloned.1.call-done = f32[32,512]{1,0:T(8,128)} async-done(((f32[32,512]{1,0:T(8,128)}), f32[32,512]{1,0:T(8,128)}) %all-reduce.3.cloned.1.call-update) | async-done | bytes 65552 | tf_op jit(solution)/shard_map/psum | solution.py:202
  376.5 0.9 fusion.102
  378.1 1.1 convolution_bitcast_fusion.1
  379.2 1.1 add_select_fusion.22
  380.3 1.1 copy.355
  383.5 212.7 %reduce-scatter.3.cloned.1.call-done = f32[32,128]{1,0:T(8,128)} async-done(((f32[32,4096]{1,0:T(8,128)}), f32[32,128]{1,0:T(8,128)}) %reduce-scatter.3.cloned.1.call-update) | async-done | bytes 16400 | tf_op jit(solution)/shard_map/reduce_scatter | solution.py:204
  596.2 0.7 fusion.339
  597.5 196.9 %psum.43 = f32[2,2,32,32]{2,3,1,0:T(8,128)S(1)} all-reduce(f32[2,2,32,32]{2,3,1,0:T(8,128)S(1)} %pad_maximum_fusion.2), channel_id=1, replica_groups=mesh['row'=32,'col'=16] {'row'}, use_global_device_ids=true, to_apply=%region_2.4 | all-reduce | flops 4096 | bytes 32768 | tf_op jit(solution)/shard_map/psum | solution.py:207
  794.4 163.6 %psum.44 = f32[2,2,32,32]{2,3,1,0:T(8,128)S(1)} all-reduce(f32[2,2,32,32]{2,3,1,0:T(8,128)S(1)} %psum.43), channel_id=1, replica_groups=mesh['row'=32,'col'=16] {'col'}, use_global_device_ids=true, to_apply=%region_3.5 | all-reduce | flops 4096 | bytes 32768 | tf_op jit(solution)/shard_map/psum | solution.py:206
  958.0 403.5 %while.36 = (s32[]{:T(128)}, f32[32,64]{0,1:T(8,128)S(1)}, s32[]{:T(128)}, s32[]{:T(128)}, s32[]{:T(128)}, /*index=5*/s32[]{:T(128)}, s32[]{:T(128)}, f32[]{:T(128)}, f32[]{:T(128)}, f32[]{:T(128)}, /*index=10*/f32[]{:T(128)}) while((s32[]{:T(128)}, f32[32,64]{0,1:T(8,128)S(1)}, s32[]{:T(128)}, s32[]{:T(128)}, ...), condition=%wide.region_7.9_spmd.clone.clone, body=%wide.region_4.8_spmd.clone.clone.sunk | while | flops 87498 | bytes 50118 | solution.py:82
  958.7 0.7 iota_reduce_fusion.4
  971.3 0.7 iota_reduce_fusion.4
  983.9 0.7 iota_reduce_fusion.4
  996.5 0.7 iota_reduce_fusion.4
  1009.1 0.7 iota_reduce_fusion.4
  1021.7 0.7 iota_reduce_fusion.4
  1034.4 0.7 iota_reduce_fusion.4
  1047.0 0.7 iota_reduce_fusion.4
  1059.6 0.7 iota_reduce_fusion.4
  1072.2 0.7 iota_reduce_fusion.4
  1084.8 0.7 iota_reduce_fusion.4
  1097.4 0.7 iota_reduce_fusion.4
  1110.0 0.7 iota_reduce_fusion.4
  1173.0 0.7 iota_reduce_fusion.4
  1185.7 0.7 iota_reduce_fusion.4
  1198.3 0.7 iota_reduce_fusion.4
  1210.9 0.7 iota_reduce_fusion.4
  1223.5 0.7 iota_reduce_fusion.4
  1236.1 0.7 iota_reduce_fusion.4
  1248.7 0.7 iota_reduce_fusion.4
  1261.3 0.7 iota_reduce_fusion.4
  1273.9 0.7 iota_reduce_fusion.4
  1364.9 100.5 %all_gather.7 = f32[32,4096]{1,0:T(8,128)S(1)} all-gather(f32[32,128]{1,0:T(8,128)S(1)} %get-tuple-element.280), channel_id=1, replica_groups=mesh['row'=32,'col'=16] {'row'}, dimensions={1}, use_global_device_ids=true | all-gather | bytes 540672 | tf_op jit(solution)/shard_map/all_gather | solution.py:201
  1466.7 0.8 copy_bitcast_fusion.6
  1468.0 265.4 %all-reduce.5.cloned.1.call-done = f32[32,512]{1,0:T(8,128)} async-done(((f32[32,512]{1,0:T(8,128)}), f32[32,512]{1,0:T(8,128)}) %all-reduce.5.cloned.1.call-update) | async-done | bytes 65552 | tf_op jit(solution)/shard_map/psum | solution.py:202
  1733.5 0.9 fusion.103
  1734.6 1.1 convolution_bitcast_fusion
  1735.7 1.1 add_select_fusion.18
  1736.8 1.1 copy.354
  1739.3 213.3 %reduce-scatter.5.cloned.1.call-done = f32[32,128]{1,0:T(8,128)} async-done(((f32[32,4096]{1,0:T(8,128)}), f32[32,128]{1,0:T(8,128)}) %reduce-scatter.5.cloned.1.call-update) | async-done | bytes 16400 | tf_op jit(solution)/shard_map/reduce_scatter | solution.py:204
  1952.6 0.7 fusion.343
  1953.9 196.9 %psum.46 = f32[2,2,32,32]{2,3,1,0:T(8,128)S(1)} all-reduce(f32[2,2,32,32]{2,3,1,0:T(8,128)S(1)} %pad_maximum_fusion.3), channel_id=1, replica_groups=mesh['row'=32,'col'=16] {'row'}, use_global_device_ids=true, to_apply=%region_10.12 | all-reduce | flops 4096 | bytes 32768 | tf_op jit(solution)/shard_map/psum | solution.py:207
  2150.8 163.6 %psum.47 = f32[2,2,32,32]{2,3,1,0:T(8,128)S(1)} all-reduce(f32[2,2,32,32]{2,3,1,0:T(8,128)S(1)} %psum.46), channel_id=1, replica_groups=mesh['row'=32,'col'=16] {'col'}, use_global_device_ids=true, to_apply=%region_11.13 | all-reduce | flops 4096 | bytes 32768 | tf_op jit(solution)/shard_map/psum | solution.py:206
  2314.5 403.5 %while.37 = (s32[]{:T(128)}, f32[32,64]{0,1:T(8,128)S(1)}, s32[]{:T(128)}, s32[]{:T(128)}, s32[]{:T(128)}, /*index=5*/s32[]{:T(128)}, s32[]{:T(128)}, f32[]{:T(128)}, f32[]{:T(128)}, f32[]{:T(128)}, /*index=10*/f32[]{:T(128)}) while((s32[]{:T(128)}, f32[32,64]{0,1:T(8,128)S(1)}, s32[]{:T(128)}, s32[]{:T(128)}, ...), condition=%wide.region_15.17_spmd.clone.clone, body=%wide.region_12.16_spmd.clone.clone.sunk | while | flops 87498 | bytes 50118 | solution.py:82
  2315.2 0.7 iota_reduce_fusion.5
  2327.8 0.7 iota_reduce_fusion.5
  2340.4 0.7 iota_reduce_fusion.5
  2353.0 0.7 iota_reduce_fusion.5
  2365.6 0.7 iota_reduce_fusion.5
  2378.2 0.7 iota_reduce_fusion.5
  2390.8 0.7 iota_reduce_fusion.5
  2403.4 0.7 iota_reduce_fusion.5
  2542.1 0.7 iota_reduce_fusion.5
  2554.7 0.7 iota_reduce_fusion.5
  2567.4 0.7 iota_reduce_fusion.5
  2580.0 0.7 iota_reduce_fusion.5
  2592.6 0.7 iota_reduce_fusion.5
  2605.2 0.7 iota_reduce_fusion.5
  2617.8 0.7 iota_reduce_fusion.5
  2630.4 0.7 iota_reduce_fusion.5
  2643.0 0.7 iota_reduce_fusion.5
  (676 shorter events, 157.1 us)
Async XLA Ops:
  7.2 116.5 %copy-start = (s32[4,4,128,128]{3,2,1,0:T(8,128)S(1)}, s32[4,4,128,128]{3,2,1,0:T(8,128)}, u32[]{:S(2)}) copy-start(s32[4,4,128,128]{3,2,1,0:T(8,128)} %param.15) | copy-start | bytes 3145732
  7.2 369.3 %all-reduce.3.cloned.1.call-start = ((), (), s32[]{:S(2)}) async-start(), calls=%async_computation.2 | async-start | bytes 131072 | tf_op jit(solution)/shard_map/psum | solution.py:202
  125.7 0.7 copy-start.5
  125.7 0.8 copy-start.6
  125.7 470.4 %reduce-scatter.3.cloned.1.call-start = ((), (), s32[]{:S(2)}) async-start(), calls=%async_computation.3 | async-start | bytes 540672 | tf_op jit(solution)/shard_map/reduce_scatter | solution.py:204
  126.9 0.7 copy-start.7
  128.2 0.7 copy-start.8
  377.4 0.7 copy-start.4
  381.5 1352.0 %all-reduce.5.cloned.1.call-start = ((), (), s32[]{:S(2)}) async-start(), calls=%async_computation.4 | async-start | bytes 131072 | tf_op jit(solution)/shard_map/psum | solution.py:202
  382.0 0.7 copy-start.9
  382.0 0.7 copy-start.10
  382.8 0.7 copy-start.1
  1364.1 0.7 copy-start.2
  1467.5 485.1 %reduce-scatter.5.cloned.1.call-start = ((), (), s32[]{:S(2)}) async-start(), calls=%async_computation.5 | async-start | bytes 540672 | tf_op jit(solution)/shard_map/reduce_scatter | solution.py:204
  2719.6 0.7 copy-start.3
Sparse Core Ops, SparseCore 0:
  125.8 250.6 all-reduce.2
  381.6 214.5 reduce-scatter.2
  1467.6 265.8 all-reduce.4
  1738.1 214.5 reduce-scatter.4
